TPU v7x, 32 devices: a whole 2x2x4 slice. The times are simulated.
32 devices in a mesh: groups: 2 (over x), mp: 8 (over z, y), dp: 2 (over core).
Axes of the slice: x: 2, y: 2, z: 4, core: 2. Of those that a mesh axis runs over, the one named last changes fastest.
Arguments:
- latents: bfloat16 [12, 128, 128, 320], P(('groups', 'dp'), 'mp'), parts along dimension 0, may hold values from -6 to 6
- room_labels: int32 [12, 128, 128], P(('groups', 'dp'), 'mp'), parts along dimension 0, may hold values from 0 to 15
- timesteps: int32 [12], P(('groups', 'dp')), parts along dimension 0, may hold values from 0 to 999
- label_table: bfloat16 [16, 320], replicated, may hold values from -6 to 6
- time_weight: bfloat16 [1280, 320], replicated, may hold values from -0.15625 to 0.15625
- trunk_weight: bfloat16 [320, 3, 3, 320], P('mp'), may hold values from -0.109375 to 0.109375
- control_weight: bfloat16 [320, 3, 3, 320], P('mp'), may hold values from -0.109375 to 0.109375
- mix_weight: bfloat16 [320, 320], P('mp'), may hold values from -0.3125 to 0.3125
- cotangent: bfloat16 [12, 128, 128, 320], P(('groups', 'dp'), 'mp'), parts along dimension 0, may hold values from -0.08984375 to 0.08984375
Outputs:
- output: bfloat16 [12, 128, 128, 320], P(('groups', 'dp'), 'mp'), parts along dimension 0
- grad_control: float32 [640, 3, 3, 320], P(('groups', 'mp')), parts along dimension 0
- grad_mix: float32 [640, 320], P(('groups', 'mp')), parts along dimension 0
- grad_table: float32 [32, 320], P('groups'), parts along dimension 0
There are 2 independent parts, one for each index of `groups`. A program takes and returns all parts, laid end to end along the dimension named above; an argument that names none is the same for every part. Nothing has to cross between parts.
All inputs are finite; a program needn't handle non-finite values.
Results may differ from a plain program's by a relative error of at most 0.0057.
Values may be sent and summed in bfloat16 or wider, within the bound.
A program may use at most 256 MiB of HBM per device.

v0:
```python
import math
import jax
import jax.numpy as jnp
from jax import lax
from jax.sharding import PartitionSpec as P


def with_halo(cells, sides, width):
    for axis, dim in sides:
        count = lax.axis_size(axis)
        ends = count - 1
        head = lax.slice_in_dim(cells, 0, width, axis=dim)
        tail = lax.slice_in_dim(cells, cells.shape[dim] - width, cells.shape[dim], axis=dim)
        cells = jnp.concatenate(
            [
                lax.ppermute(tail, axis, [(i, (i + 1) % count) for i in range(ends)]),
                cells,
                lax.ppermute(head, axis, [((i + 1) % count, i) for i in range(ends)]),
            ],
            axis=dim,
        )
    return cells


def sinusoid(timesteps, embed_width):
    half_width = embed_width // 2
    indices = jnp.arange(half_width, dtype=jnp.float32)
    frequency = jnp.exp(-math.log(10000.0) * indices / half_width)
    angles = timesteps.astype(jnp.float32)[:, None] * frequency[None, :]
    return jnp.concatenate([jnp.cos(angles), jnp.sin(angles)], axis=1)


def forward_taps(frame, kernel):
    row_count = frame.shape[1] - 2
    span_cols = frame.shape[2] - 2
    running = jnp.zeros(frame.shape[:1] + (row_count, span_cols, kernel.shape[3]), jnp.float32)
    for tap_row in range(3):
        for tap_col in range(3):
            running = running + jnp.einsum(
                "bhwc,cd->bhwd",
                frame[:, tap_row : tap_row + row_count, tap_col : tap_col + span_cols],
                kernel[:, tap_row, tap_col],
                preferred_element_type=jnp.float32,
            )
    return running


def backward_taps(frame, kernel):
    row_count = frame.shape[1] - 2
    span_cols = frame.shape[2] - 2
    running = jnp.zeros(frame.shape[:1] + (row_count, span_cols, kernel.shape[0]), jnp.float32)
    for tap_row in range(3):
        for tap_col in range(3):
            running = running + jnp.einsum(
                "bhwd,cd->bhwc",
                frame[
                    :, 2 - tap_row : 2 - tap_row + row_count, 2 - tap_col : 2 - tap_col + span_cols
                ],
                kernel[:, tap_row, tap_col],
                preferred_element_type=jnp.float32,
            )
    return running


def per_device(
    latents,
    room_labels,
    timesteps,
    label_table,
    time_weight,
    trunk_weight,
    control_weight,
    mix_weight,
    cotangent,
):
    images, row_count, span_cols, channels = latents.shape
    rooms = label_table.shape[0]
    onehot = (room_labels[..., None] == jnp.arange(rooms, dtype=jnp.int32)).astype(jnp.bfloat16)
    embedded = jnp.einsum("bhwr,rc->bhwc", onehot, label_table, preferred_element_type=jnp.float32)
    control_in = (latents.astype(jnp.float32) + embedded).astype(jnp.bfloat16)
    stacked = jnp.stack([latents, control_in])
    framed = with_halo(stacked, (("mp", 2),), 1)
    framed = jnp.pad(framed, ((0, 0), (0, 0), (0, 0), (1, 1), (0, 0)))
    trunk_frame = framed[0]
    control_frame = framed[1]
    time_features = jax.nn.silu(sinusoid(timesteps, time_weight.shape[0])).astype(jnp.bfloat16)
    time_shift = jnp.dot(time_features, time_weight, preferred_element_type=jnp.float32)[
        :, None, None, :
    ]
    trunk_full = lax.all_gather(trunk_weight, "mp", axis=0, tiled=True)
    trunk_pre = forward_taps(trunk_frame, trunk_full) + time_shift
    control_full, mix_full = (
        lax.all_gather(control_weight, "mp", axis=0, tiled=True),
        lax.all_gather(mix_weight, "mp", axis=0, tiled=True),
    )
    control_pre = forward_taps(control_frame, control_full) + time_shift
    gated_act = jax.nn.silu(control_pre).astype(jnp.bfloat16)
    mixed_out = jnp.einsum("bhwc,cd->bhwd", gated_act, mix_full, preferred_element_type=jnp.float32)
    output = (jax.nn.silu(trunk_pre) + mixed_out).astype(jnp.bfloat16)
    back_gate = jnp.einsum("bhwd,cd->bhwc", cotangent, mix_full, preferred_element_type=jnp.float32)
    sigmoid_val = jax.nn.sigmoid(control_pre)
    back_pre = (back_gate * sigmoid_val * (1.0 + control_pre * (1.0 - sigmoid_val))).astype(
        jnp.bfloat16
    )
    back_frame = with_halo(back_pre, (("mp", 1),), 1)
    back_frame = jnp.pad(back_frame, ((0, 0), (0, 0), (1, 1), (0, 0)))
    back_kernel = lax.all_gather(control_weight, "mp", axis=0, tiled=True)
    back_in = backward_taps(back_frame, back_kernel)
    table_local = jnp.einsum(
        "bhwr,bhwc->rc", onehot.astype(jnp.float32), back_in, precision=lax.Precision.HIGHEST
    )
    grad_table = lax.psum(table_local, ("mp", "dp"))
    pieces = []
    for tap_row in range(3):
        for tap_col in range(3):
            pieces.append(
                jnp.einsum(
                    "bhwc,bhwd->cd",
                    control_frame[:, tap_row : tap_row + row_count, tap_col : tap_col + span_cols],
                    back_pre,
                    preferred_element_type=jnp.float32,
                )
            )
    kernel_rows = jnp.stack(pieces, axis=1).reshape(channels, 9 * channels)
    mix_rows = jnp.einsum("bhwc,bhwd->cd", gated_act, cotangent, preferred_element_type=jnp.float32)
    grad_term = jnp.concatenate([kernel_rows, mix_rows], axis=1)
    grad_rows = lax.psum_scatter(grad_term, "mp", scatter_dimension=0, tiled=True)
    grad_rows = lax.psum(grad_rows, "dp")
    grad_control = grad_rows[:, : 9 * channels].reshape(grad_rows.shape[0], 3, 3, channels)
    grad_mix = grad_rows[:, 9 * channels :]
    return (output, grad_control, grad_mix, grad_table)


def solution(mesh):
    in_specs = (
        P(("groups", "dp"), "mp", None, None),
        P(("groups", "dp"), "mp", None),
        P(("groups", "dp")),
        P(),
        P(),
        P("mp", None, None, None),
        P("mp", None, None, None),
        P("mp", None),
        P(("groups", "dp"), "mp", None, None),
    )
    out_specs = (
        P(("groups", "dp"), "mp", None, None),
        P(("groups", "mp"), None, None, None),
        P(("groups", "mp"), None),
        P("groups", None),
    )
    return jax.shard_map(
        per_device, mesh=mesh, in_specs=in_specs, out_specs=out_specs, check_vma=False
    )
```

profile of v0, /device:TPU:0, one launch (start us, length us, event | category | flops | bytes accessed | tf_op | source)
XLA Modules:
  0.0 456.9 jit_solution(16254729280796380880)
XLA Ops:
  19.7 49.6 %all_gather.12 = bf16[320,320]{1,0:T(8,128)(2,1)S(1)} all-gather(bf16[40,320]{1,0:T(8,128)(2,1)S(1)} %copy-done.13), channel_id=1, replica_groups=mesh['groups'=2,'mp'=8,'dp'=2] {'mp'}, dimensions={0}, use_global_device_ids=true | all-gather | bytes 230400 | tf_op jit(solution)/shard_map/all_gather | solution.py:94
  69.9 18.2 %select_maximum_fusion = bf16[2,3,18,130,320]{3,4,2,1,0:T(8,128)(2,1)S(1)} fusion(bf16[2,3,1,128,320]{3,4,2,1,0:T(8,128)(2,1)S(1)} %collective-permute-done.1, bf16[2,3,1,128,320]{3,4,2,1,0:T(8,128)(2,1)S(1)} %collective-permute-done, bf16[1,3,16,128,320]{3,4,2,1,0:T(8,128)(2,1)} %copy-done.6, bf16[1,3,16,128,320]{3,4,2,1,0:T(8,128)(2,1)} %bitcast.302), kind=kLoop, calls=%fused_computation.5 | loop fusion | flops 67392000 | bytes 17832960 | tf_op jit(solution)/shard_map/concatenate | solution.py:14
  88.1 6.6 %slice_bitcast_fusion.1 = (bf16[3,18,130,320]{2,3,1,0:T(8,128)(2,1)}, bf16[3,18,130,320]{2,3,1,0:T(8,128)(2,1)}) fusion(bf16[2,3,18,130,320]{3,4,2,1,0:T(8,128)(2,1)S(1)} %select_maximum_fusion), kind=kLoop, calls=%fused_computation.17 | loop fusion | bytes 17971200 | tf_op jit(solution)/shard_map/squeeze | solution.py:84
  94.7 9.1 %fusion.64 = f32[3,16,128,320]{2,3,1,0:T(8,128)} fusion(bf16[3,18,130,320]{2,3,1,0:T(8,128)(2,1)} %get-tuple-element.13, bf16[320,3,3,320]{3,0,2,1:T(8,128)(2,1)} %all-gather.5.cloned.1.call-done), kind=kOutput, calls=%fused_computation.79 | convolution fusion | flops 1258291200 | bytes 12042240 | tf_op jit(solution)/shard_map/bhwc,cd->bhwd/dot_general | solution.py:39
  114.6 5.5 %fusion.76 = f32[3,16,128,320]{2,3,1,0:T(8,128)} fusion(bf16[3,18,130,320]{2,3,1,0:T(8,128)(2,1)S(1)} %copy-done.2, bf16[320,3,3,320]{3,0,2,1:T(8,128)(2,1)S(1)} %copy-done.9), kind=kOutput, calls=%fused_computation.91 | convolution fusion | flops 1258291200 | bytes 12042240 | tf_op jit(solution)/shard_map/bhwc,cd->bhwd/dot_general | solution.py:39
  125.5 5.8 %fusion.84 = f32[3,16,128,320]{2,3,1,0:T(8,128)} fusion(bf16[3,18,130,320]{2,3,1,0:T(8,128)(2,1)S(1)} %copy-done.2, bf16[320,3,3,320]{3,0,2,1:T(8,128)(2,1)S(1)} %copy-done.9), kind=kOutput, calls=%fused_computation.99 | convolution fusion | flops 1258291200 | bytes 12042240 | tf_op jit(solution)/shard_map/bhwc,cd->bhwd/dot_general | solution.py:39
  131.3 5.7 %fusion.88 = f32[3,16,128,320]{2,3,1,0:T(8,128)} fusion(bf16[3,18,130,320]{2,3,1,0:T(8,128)(2,1)S(1)} %copy-done.2, bf16[320,3,3,320]{3,0,2,1:T(8,128)(2,1)S(1)} %copy-done.9), kind=kOutput, calls=%fused_computation.103 | convolution fusion | flops 1258291200 | bytes 12042240 | tf_op jit(solution)/shard_map/bhwc,cd->bhwd/dot_general | solution.py:39
  142.4 28.2 %multiply_convert_fusion.1 = (bf16[3,16,128,320]{2,3,1,0:T(8,128)(2,1)}, f32[3,16,128,320]{2,3,1,0:T(8,128)}) fusion(f32[3,320]{1,0:T(4,128)S(1)} %fusion.163, bf16[3,18,130,320]{2,3,1,0:T(8,128)(2,1)} %get-tuple-element.13, bf16[320,3,3,320]{3,0,2,1:T(8,128)(2,1)S(1)} %copy-done.9, f32[3,16,128,320]{2,3,1,0:T(8,128)} %fusion.64, ...), kind=kOutput, calls=%fused_computation.29 | convolution fusion | flops 1285816320 | bytes 78895104 | tf_op jit(solution)/shard_map/bhwc,cd->bhwd/dot_general | solution.py:39
  170.6 7.3 %multiply_convert_fusion = bf16[3,16,128,320]{2,3,1,0:T(8,128)(2,1)S(1)} fusion(f32[3,16,128,320]{2,3,1,0:T(8,128)} %get-tuple-element.21, bf16[3,16,128,320]{2,3,1,0:T(8,128)(2,1)} %param.17, bf16[320,320]{1,0:T(8,128)(2,1)S(1)} %all_gather.12), kind=kOutput, calls=%fused_computation.27 | convolution fusion | flops 1275985920 | bytes 15933440 | tf_op jit(solution)/shard_map/bhwd,cd->bhwc/dot_general | solution.py:100
  178.0 5.7 %fusion.101 = f32[320,9,320]{0,2,1:T(8,128)S(1)} fusion(bf16[3,16,128,320]{2,3,1,0:T(8,128)(2,1)S(1)} %multiply_convert_fusion, bf16[3,18,130,320]{2,3,1,0:T(8,128)(2,1)} %get-tuple-element.13), kind=kOutput, calls=%fused_computation.110 | convolution fusion | flops 1258291200 | bytes 8355840 | tf_op jit(solution)/shard_map/bhwc,bhwd->cd/dot_general | solution.py:117
  210.8 5.6 %copy.38 = f32[320,2880]{1,0:T(8,128)} copy(f32[320,2880]{0,1:T(8,128)} %bitcast.304) | data formatting | bytes 7372800 | tf_op jit(solution)/shard_map/reshape | solution.py:124
  216.4 7.6 %fusion.156 = f32[3,16,128,320]{2,3,1,0:T(8,128)} fusion(bf16[3,16,128,320]{2,3,1,0:T(8,128)(2,1)} %get-tuple-element.20, bf16[320,320]{1,0:T(8,128)(2,1)S(1)} %all_gather.12), kind=kOutput, calls=%fused_computation.151 | convolution fusion | flops 1258291200 | bytes 12001280 | tf_op jit(solution)/shard_map/bhwc,cd->bhwd/dot_general | solution.py:98
  228.7 9.0 %fusion.42 = f32[3,16,128,320]{2,3,1,0:T(8,128)} fusion(bf16[3,18,130,320]{2,3,1,0:T(8,128)(2,1)} %get-tuple-element.12, bf16[320,3,3,320]{3,0,2,1:T(8,128)(2,1)} %all-gather.3.cloned.1.call-done), kind=kOutput, calls=%fused_computation.57 | convolution fusion | flops 1258291200 | bytes 12042240 | tf_op jit(solution)/shard_map/bhwc,cd->bhwd/dot_general | solution.py:39
  237.7 7.5 %fusion.44 = f32[3,16,128,320]{2,3,1,0:T(8,128)} fusion(bf16[3,18,130,320]{2,3,1,0:T(8,128)(2,1)} %get-tuple-element.12, bf16[320,3,3,320]{3,0,2,1:T(8,128)(2,1)S(1)} %copy-done.11), kind=kOutput, calls=%fused_computation.59 | convolution fusion | flops 1258291200 | bytes 12042240 | tf_op jit(solution)/shard_map/bhwc,cd->bhwd/dot_general | solution.py:39
  250.7 5.6 %fusion.48 = f32[3,16,128,320]{2,3,1,0:T(8,128)} fusion(bf16[3,18,130,320]{2,3,1,0:T(8,128)(2,1)S(1)} %bitcast.299, bf16[320,3,3,320]{3,0,2,1:T(8,128)(2,1)S(1)} %copy-done.11), kind=kOutput, calls=%fused_computation.63 | convolution fusion | flops 1258291200 | bytes 12042240 | tf_op jit(solution)/shard_map/bhwc,cd->bhwd/dot_general | solution.py:39
  261.6 6.0 %fusion.52 = f32[3,16,128,320]{2,3,1,0:T(8,128)} fusion(bf16[3,18,130,320]{2,3,1,0:T(8,128)(2,1)S(1)} %bitcast.299, bf16[320,3,3,320]{3,0,2,1:T(8,128)(2,1)S(1)} %copy-done.11), kind=kOutput, calls=%fused_computation.67 | convolution fusion | flops 1258291200 | bytes 12042240 | tf_op jit(solution)/shard_map/bhwc,cd->bhwd/dot_general | solution.py:39
  267.6 5.6 %fusion.54 = f32[3,16,128,320]{2,3,1,0:T(8,128)} fusion(bf16[3,18,130,320]{2,3,1,0:T(8,128)(2,1)S(1)} %bitcast.299, bf16[320,3,3,320]{3,0,2,1:T(8,128)(2,1)S(1)} %copy-done.11), kind=kOutput, calls=%fused_computation.69 | convolution fusion | flops 1258291200 | bytes 12042240 | tf_op jit(solution)/shard_map/bhwc,cd->bhwd/dot_general | solution.py:39
  278.5 28.6 %add_convert_fusion = bf16[3,16,128,320]{2,3,1,0:T(8,128)(2,1)} fusion(f32[3,16,128,320]{2,3,1,0:T(8,128)} %fusion.156, f32[3,16,128,320]{2,3,1,0:T(8,128)} %fusion.42, f32[3,16,128,320]{2,3,1,0:T(8,128)} %fusion.44, f32[3,16,128,320]{2,3,1,0:T(8,128)} %fusion.46, f32[3,16,128,320]{2,3,1,0:T(8,128)} %fusion.48, f32[3,16,128,320]{2,3,1,0:T(8,128)} %fusion.50, ...), kind=kOutput, calls=%fused_computation.28 | convolution fusion | flops 1287782400 | bytes 78892800 | tf_op jit(solution)/shard_map/bhwc,cd->bhwd/dot_general | solution.py:39
  307.2 7.6 %fusion.158 = f32[3,16,128,320]{2,3,1,0:T(8,128)} fusion(bf16[3,16,128,320]{2,3,1,0:T(8,128)(2,1)} %copy-done.3, bf16[320,3,3,320]{3,0,2,1:T(8,128)(2,1)S(1)} %copy-done.9), kind=kOutput, calls=%fused_computation.153 | convolution fusion | flops 1258291200 | bytes 12042240 | tf_op jit(solution)/shard_map/bhwd,cd->bhwc/dot_general | solution.py:54
  325.4 6.3 %fusion.9 = bf16[3,18,130,320]{2,3,1,0:T(8,128)(2,1)S(1)} fusion(bf16[3,1,128,320]{2,3,1,0:T(8,128)(2,1)S(1)} %collective-permute-done.3, bf16[3,16,128,320]{2,3,1,0:T(8,128)(2,1)S(1)} %copy-done.4, bf16[3,1,128,320]{2,3,1,0:T(8,128)(2,1)S(1)} %collective-permute-done.2), kind=kLoop, calls=%fused_computation.15 | loop fusion | flops 26956800 | bytes 8916480 | tf_op jit(solution)/shard_map/concatenate | solution.py:14
  331.8 5.5 %fusion.30 = f32[3,16,128,320]{2,3,1,0:T(8,128)} fusion(bf16[3,18,130,320]{2,3,1,0:T(8,128)(2,1)S(1)} %fusion.9, bf16[320,3,3,320]{3,0,2,1:T(8,128)(2,1)S(1)} %copy-done.9), kind=kOutput, calls=%fused_computation.45 | convolution fusion | flops 1258291200 | bytes 12042240 | tf_op jit(solution)/shard_map/bhwd,cd->bhwc/dot_general | solution.py:54
  342.7 5.5 %fusion.34 = f32[3,16,128,320]{2,3,1,0:T(8,128)} fusion(bf16[3,18,130,320]{2,3,1,0:T(8,128)(2,1)S(1)} %fusion.9, bf16[320,3,3,320]{3,0,2,1:T(8,128)(2,1)S(1)} %copy-done.9), kind=kOutput, calls=%fused_computation.49 | convolution fusion | flops 1258291200 | bytes 12042240 | tf_op jit(solution)/shard_map/bhwd,cd->bhwc/dot_general | solution.py:54
  364.4 24.3 %fusion.152 = f32[16,320]{1,0:T(8,128)S(1)} fusion(f32[3,16,128,320]{2,3,1,0:T(8,128)} %fusion.28, f32[3,16,128,320]{2,3,1,0:T(8,128)} %fusion.23, f32[3,16,128,320]{2,3,1,0:T(8,128)} %fusion.30, f32[3,16,128,320]{2,3,1,0:T(8,128)} %fusion.32, f32[3,16,128,320]{2,3,1,0:T(8,128)} %fusion.158, f32[3,16,128,320]{2,3,1,0:T(8,128)} %fusion.34, ...), kind=kOutput, calls=%fused_computation.128 | convolution fusion | flops 393314304 | bytes 70823936 | tf_op jit(solution)/shard_map/bhwr,bhwc->rc/dot_general | solution.py:109
  388.7 57.6 %psum.15 = f32[16,320]{1,0:T(8,128)} all-reduce(f32[16,320]{1,0:T(8,128)S(1)} %fusion.152), channel_id=1, replica_groups=mesh['groups'=2,'mp'=8,'dp'=2] {'mp','dp'}, use_global_device_ids=true, to_apply=%region_2.3 | all-reduce | flops 5120 | bytes 40960 | tf_op jit(solution)/shard_map/psum | solution.py:112
  (100 shorter events, 118.2 us)
Async XLA Ops:
  7.2 62.4 %copy-start = (bf16[1280,320]{0,1:T(8,128)(2,1)S(1)}, bf16[1280,320]{0,1:T(8,128)(2,1)}, u32[]{:S(2)}) copy-start(bf16[1280,320]{0,1:T(8,128)(2,1)} %param.13) | copy-start | bytes 2457604
  7.2 87.5 %all-gather.5.cloned.1.call-start = ((), (), s32[]{:S(2)}) async-start(), calls=%async_computation.2 | async-start | bytes 2488320 | tf_op jit(solution)/shard_map/all_gather | solution.py:93
  7.9 11.8 %copy-start.13 = (bf16[40,320]{1,0:T(8,128)(2,1)S(1)}, bf16[40,320]{1,0:T(8,128)(2,1)}, u32[]{:S(2)}) copy-start(bf16[40,320]{1,0:T(8,128)(2,1)} %param.16) | copy-start | bytes 76804
  7.9 61.5 %copy-start.15 = (s32[3]{0:T(128)S(1)}, s32[3]{0:T(128)}, u32[]{:S(2)}) copy-start(s32[3]{0:T(128)} %param.11) | copy-start | bytes 40
  7.9 220.7 %all-gather.3.cloned.1.call-start = ((), (), s32[]{:S(2)}) async-start(), calls=%async_computation.1 | async-start | bytes 2488320 | tf_op jit(solution)/shard_map/all_gather | solution.py:90
  13.5 56.4 %collective-permute-start = (bf16[2,3,1,128,320]{3,4,2,1,0:T(8,128)(2,1)S(1)}, bf16[2,3,1,128,320]{3,4,2,1,0:T(8,128)(2,1)S(1)}, u32[]{:S(2)}, u32[]{:S(2)}) collective-permute-start(bf16[2,3,1,128,320]{3,4,2,1,0:T(8,128)(2,1)S(1)} %get-tuple-element.14), channel_id=1, source_target_pairs={{0,2},{2,4},{4,6},{6,8},{8,10},{10,12},{12,14},{1,3},{3,5},{5,7},{... | collective-permute-start | bytes 1474568 | tf_op jit(solution)/shard_map/ppermute | solution.py:16
  18.3 51.5 %collective-permute-start.1 = (bf16[2,3,1,128,320]{3,4,2,1,0:T(8,128)(2,1)S(1)}, bf16[2,3,1,128,320]{3,4,2,1,0:T(8,128)(2,1)S(1)}, u32[]{:S(2)}, u32[]{:S(2)}) collective-permute-start(bf16[2,3,1,128,320]{3,4,2,1,0:T(8,128)(2,1)S(1)} %get-tuple-element.15), channel_id=1, source_target_pairs={{2,0},{4,2},{6,4},{8,6},{10,8},{12,10},{14,12},{3,1},{5,3},{7,5},{... | collective-permute-start | bytes 1474568 | tf_op jit(solution)/shard_map/ppermute | solution.py:18
  19.7 344.7 %reduce-scatter.4.cloned.1.call-start = ((), (), s32[]{:S(2)}) async-start(), calls=%async_computation.4 | async-start | bytes 4608000
  94.7 9.1 %copy-start.2 = (bf16[3,18,130,320]{2,3,1,0:T(8,128)(2,1)S(1)}, bf16[3,18,130,320]{2,3,1,0:T(8,128)(2,1)}, u32[]{:S(2)}) copy-start(bf16[3,18,130,320]{2,3,1,0:T(8,128)(2,1)} %get-tuple-element.13) | copy-start | bytes 13478404
  94.7 9.1 %copy-start.9 = (bf16[320,3,3,320]{3,0,2,1:T(8,128)(2,1)S(1)}, bf16[320,3,3,320]{3,0,2,1:T(8,128)(2,1)}, u32[]{:S(2)}) copy-start(bf16[320,3,3,320]{3,0,2,1:T(8,128)(2,1)} %all-gather.5.cloned.1.call-done) | copy-start | bytes 5529604
  177.9 28.4 %copy-start.3 = (bf16[3,16,128,320]{2,3,1,0:T(8,128)(2,1)}, bf16[3,16,128,320]{2,3,1,0:T(8,128)(2,1)S(1)}, u32[]{:S(2)}) copy-start(bf16[3,16,128,320]{2,3,1,0:T(8,128)(2,1)S(1)} %multiply_convert_fusion) | copy-start | bytes 11796484
  178.0 14.5 %slice-start.3 = ((s8[8847360]{0:T(1024)(128)(4,1)}), s8[4194304]{0:T(1024)(128)(4,1)S(1)}, s32[]{:S(2)}) async-start(s8[8847360]{0:T(1024)(128)(4,1)} %bitcast.300), calls=%async_computation.8 | async-start | bytes 8388608
  178.0 14.5 %slice-start.4 = ((s8[8847360]{0:T(1024)(128)(4,1)}), s8[4194304]{0:T(1024)(128)(4,1)S(1)}, s32[]{:S(2)}) async-start(s8[8847360]{0:T(1024)(128)(4,1)} %bitcast.300), calls=%async_computation.9 | async-start | bytes 8388608
  183.7 136.3 %collective-permute-start.2 = (bf16[3,1,128,320]{2,3,1,0:T(8,128)(2,1)S(1)}, bf16[3,1,128,320]{2,3,1,0:T(8,128)(2,1)S(1)}, u32[]{:S(2)}, u32[]{:S(2)}) collective-permute-start(bf16[3,1,128,320]{2,3,1,0:T(8,128)(2,1)S(1)} %get-tuple-element.16), channel_id=1, source_target_pairs={{0,2},{2,4},{4,6},{6,8},{8,10},{10,12},{12,14},{1,3},{3,5},{5,7},{... | collective-permute-start | bytes 737288 | tf_op jit(solution)/shard_map/ppermute | solution.py:16
  185.1 129.7 %collective-permute-start.3 = (bf16[3,1,128,320]{2,3,1,0:T(8,128)(2,1)S(1)}, bf16[3,1,128,320]{2,3,1,0:T(8,128)(2,1)S(1)}, u32[]{:S(2)}, u32[]{:S(2)}) collective-permute-start(bf16[3,1,128,320]{2,3,1,0:T(8,128)(2,1)S(1)} %get-tuple-element.17), channel_id=1, source_target_pairs={{2,0},{4,2},{6,4},{8,6},{10,8},{12,10},{14,12},{3,1},{5,3},{7,5},{... | collective-permute-start | bytes 737288 | tf_op jit(solution)/shard_map/ppermute | solution.py:18
  216.4 7.6 %copy-start.7 = (bf16[3,16,128,320]{2,3,1,0:T(8,128)(2,1)S(1)}, bf16[3,16,128,320]{2,3,1,0:T(8,128)(2,1)}, u32[]{:S(2)}) copy-start(bf16[3,16,128,320]{2,3,1,0:T(8,128)(2,1)} %get-tuple-element.20) | copy-start | bytes 11796484
  216.4 7.6 %copy-start.14 = (bf16[3,16,128,320]{2,3,1,0:T(8,128)(2,1)S(1)}, bf16[3,16,128,320]{2,3,1,0:T(8,128)(2,1)}, u32[]{:S(2)}) copy-start(bf16[3,16,128,320]{2,3,1,0:T(8,128)(2,1)} %param.17) | copy-start | bytes 11796484
  228.6 217.7 %all-reduce.5.cloned.1.call-start = ((), (), s32[]{:S(2)}) async-start(), calls=%async_computation.3 | async-start | bytes 1024000 | tf_op jit(solution)/shard_map/psum | solution.py:128
  228.7 9.0 %copy-start.11 = (bf16[320,3,3,320]{3,0,2,1:T(8,128)(2,1)S(1)}, bf16[320,3,3,320]{3,0,2,1:T(8,128)(2,1)}, u32[]{:S(2)}) copy-start(bf16[320,3,3,320]{3,0,2,1:T(8,128)(2,1)} %all-gather.3.cloned.1.call-done) | copy-start | bytes 5529604
  228.7 16.5 %slice-start = ((s8[8847360]{0:T(1024)(128)(4,1)}), s8[4194304]{0:T(1024)(128)(4,1)S(1)}, s32[]{:S(2)}) async-start(s8[8847360]{0:T(1024)(128)(4,1)} %bitcast.298), calls=%async_computation.5 | async-start | bytes 8388608
  228.7 16.5 %slice-start.1 = ((s8[8847360]{0:T(1024)(128)(4,1)}), s8[4194304]{0:T(1024)(128)(4,1)S(1)}, s32[]{:S(2)}) async-start(s8[8847360]{0:T(1024)(128)(4,1)} %bitcast.298), calls=%async_computation.6 | async-start | bytes 8388608
  237.7 7.5 %slice-start.2 = ((s8[8847360]{0:T(1024)(128)(4,1)}), s8[458752]{0:T(1024)(128)(4,1)S(1)}, s32[]{:S(2)}) async-start(s8[8847360]{0:T(1024)(128)(4,1)} %bitcast.298), calls=%async_computation.7 | async-start | bytes 917504
  307.2 7.6 %copy-start.4 = (bf16[3,16,128,320]{2,3,1,0:T(8,128)(2,1)S(1)}, bf16[3,16,128,320]{2,3,1,0:T(8,128)(2,1)}, u32[]{:S(2)}) copy-start(bf16[3,16,128,320]{2,3,1,0:T(8,128)(2,1)} %copy-done.3) | copy-start | bytes 11796484
  364.4 85.8 %copy-start.1 = (bf16[1280,320]{0,1:T(8,128)(2,1)S(1)}, bf16[1280,320]{0,1:T(8,128)(2,1)}, u32[]{:S(2)}) copy-start(bf16[1280,320]{0,1:T(8,128)(2,1)} %param.13) | copy-start | bytes 2457604
  (6 other events, 22.7 us)
Sparse Core Ops, SparseCore 0:
  10.2 66.9 all-gather.4
  79.4 49.2 all-gather.2
  228.7 87.1 reduce-scatter.3
  364.5 20.1 all-reduce.4
where the time goes:
time: 461 us; the launch traced here: 457 us
  matrix products  278 us (60%)
  blocking collectives  107 us (23%)
  other arithmetic  27.1 us (6%)
  local copies, waits for them, and re-layouts  20.2 us (4%)
  between operations  14.4 us (3%)
  starting transfers between devices  9.53 us (2%)
    dot_general x18, matrix products, forward_taps(): jnp.einsum('bhwc,cd->bhwd', frame[:, tap_row:tap_row + row_count, tap_col...  154 us
    psum x1, blocking collectives, per_device(): grad_table = lax.psum(table_local, ('mp', 'dp'))  57.6 us
    dot_general x9, matrix products, backward_taps(): jnp.einsum('bhwd,cd->bhwc', frame[:, 2 - tap_row:2 - tap_row + row_count,...  50.8 us
    all_gather x1, blocking collectives, per_device(): lax.all_gather(mix_weight, 'mp', axis=0, tiled=True)  49.6 us
    dot_general x9, matrix products, per_device(): jnp.einsum('bhwc,bhwd->cd', control_frame[:, tap_row:tap_row + row_count,...  27.3 us
    concatenate x2, other arithmetic, with_halo(): jnp.concatenate([lax.ppermute(tail, axis, [(i, (i + 1) % count) for i in...  24.5 us
    dot_general x1, matrix products, per_device(): jnp.einsum('bhwr,bhwc->rc', onehot.astype(jnp.float32), back_in, precisio...  24.3 us
  transfers between devices with their start and end apart: 8, of which 0 were waited for; matrix products, arithmetic and copies ran while one was open for 69% of the time, Pallas kernels for 0%

commit v1 on v0

--- a/solution.py
+++ b/solution.py
@@ -3,6 +3,12 @@
 import jax.numpy as jnp
 from jax import lax
 from jax.sharding import PartitionSpec as P
+
+
+def summed_here(block, axis):
+    parts = lax.all_gather(block, axis, axis=0, tiled=False)
+    acc = parts.sum(axis=0)
+    return acc
 
 
 def with_halo(cells, sides, width):
@@ -109,7 +115,7 @@
     table_local = jnp.einsum(
         "bhwr,bhwc->rc", onehot.astype(jnp.float32), back_in, precision=lax.Precision.HIGHEST
     )
-    grad_table = lax.psum(table_local, ("mp", "dp"))
+    grad_table = summed_here(table_local, ("mp", "dp"))
     pieces = []
     for tap_row in range(3):
         for tap_col in range(3):

time: 461 us -> 426 us (0.924)
  blocking collectives: 107 us -> 71.8 us
    psum x1 -> x0, blocking collectives: 57.6 us -> none  [per_device(): grad_table = lax.psum(table_local, ('mp', 'dp'))]
    all_gather x0 -> x1, blocking collectives: none -> 22.2 us  [summed_here(): parts = lax.all_gather(block, axis, axis=0, tiled=False)]
  transfers between devices with their start and end apart: 8 -> 8, of which waited for: 0 -> 0; matrix products, arithmetic and copies ran while one was open for 69% -> 75% of each run, Pallas kernels for 0% -> 0%
where the time goes in v1:
time: 426 us; the launch traced here: 422 us
  matrix products  278 us (65%)
  blocking collectives  71.8 us (17%)
  other arithmetic  27.7 us (7%)
  local copies, waits for them, and re-layouts  20.2 us (5%)
  between operations  14.5 us (3%)
  starting transfers between devices  9.53 us (2%)
    dot_general x18, matrix products, forward_taps(): jnp.einsum('bhwc,cd->bhwd', frame[:, tap_row:tap_row + row_count, tap_col...  154 us
    dot_general x9, matrix products, backward_taps(): jnp.einsum('bhwd,cd->bhwc', frame[:, 2 - tap_row:2 - tap_row + row_count,...  50.8 us
    all_gather x1, blocking collectives, per_device(): lax.all_gather(mix_weight, 'mp', axis=0, tiled=True)  49.6 us
    dot_general x9, matrix products, per_device(): jnp.einsum('bhwc,bhwd->cd', control_frame[:, tap_row:tap_row + row_count,...  27.3 us
    concatenate x2, other arithmetic, with_halo(): jnp.concatenate([lax.ppermute(tail, axis, [(i, (i + 1) % count) for i in...  24.5 us
    dot_general x1, matrix products, per_device(): jnp.einsum('bhwr,bhwc->rc', onehot.astype(jnp.float32), back_in, precisio...  24.3 us
    all_gather x1, blocking collectives, summed_here(): parts = lax.all_gather(block, axis, axis=0, tiled=False)  22.2 us
  transfers between devices with their start and end apart: 8, of which 0 were waited for; matrix products, arithmetic and copies ran while one was open for 75% of the time, Pallas kernels for 0%

profile of v1, /device:TPU:0, one launch (start us, length us, event | category | flops | bytes accessed | tf_op | source)
XLA Modules:
  0.0 422.1 jit_solution(12087852666114908139)
XLA Ops:
  19.7 49.6 %all_gather.18 = bf16[320,320]{1,0:T(8,128)(2,1)S(1)} all-gather(bf16[40,320]{1,0:T(8,128)(2,1)S(1)} %copy-done.13), channel_id=1, replica_groups=mesh['groups'=2,'mp'=8,'dp'=2] {'mp'}, dimensions={0}, use_global_device_ids=true | all-gather | bytes 230400 | tf_op jit(solution)/shard_map/all_gather | solution.py:100
  69.9 18.2 %select_maximum_fusion = bf16[2,3,18,130,320]{3,4,2,1,0:T(8,128)(2,1)S(1)} fusion(bf16[2,3,1,128,320]{3,4,2,1,0:T(8,128)(2,1)S(1)} %collective-permute-done.1, bf16[2,3,1,128,320]{3,4,2,1,0:T(8,128)(2,1)S(1)} %collective-permute-done, bf16[1,3,16,128,320]{3,4,2,1,0:T(8,128)(2,1)} %copy-done.6, bf16[1,3,16,128,320]{3,4,2,1,0:T(8,128)(2,1)} %bitcast.303), kind=kLoop, calls=%fused_computation.5 | loop fusion | flops 67392000 | bytes 17832960 | tf_op jit(solution)/shard_map/concatenate | solution.py:20
  88.1 6.6 %slice_bitcast_fusion.1 = (bf16[3,18,130,320]{2,3,1,0:T(8,128)(2,1)}, bf16[3,18,130,320]{2,3,1,0:T(8,128)(2,1)}) fusion(bf16[2,3,18,130,320]{3,4,2,1,0:T(8,128)(2,1)S(1)} %select_maximum_fusion), kind=kLoop, calls=%fused_computation.17 | loop fusion | bytes 17971200 | tf_op jit(solution)/shard_map/squeeze | solution.py:90
  94.7 9.1 %fusion.64 = f32[3,16,128,320]{2,3,1,0:T(8,128)} fusion(bf16[3,18,130,320]{2,3,1,0:T(8,128)(2,1)} %get-tuple-element.13, bf16[320,3,3,320]{3,0,2,1:T(8,128)(2,1)} %all-gather.6.cloned.1.call-done), kind=kOutput, calls=%fused_computation.79 | convolution fusion | flops 1258291200 | bytes 12042240 | tf_op jit(solution)/shard_map/bhwc,cd->bhwd/dot_general | solution.py:45
  114.6 5.5 %fusion.76 = f32[3,16,128,320]{2,3,1,0:T(8,128)} fusion(bf16[3,18,130,320]{2,3,1,0:T(8,128)(2,1)S(1)} %copy-done.2, bf16[320,3,3,320]{3,0,2,1:T(8,128)(2,1)S(1)} %copy-done.9), kind=kOutput, calls=%fused_computation.91 | convolution fusion | flops 1258291200 | bytes 12042240 | tf_op jit(solution)/shard_map/bhwc,cd->bhwd/dot_general | solution.py:45
  125.5 5.8 %fusion.84 = f32[3,16,128,320]{2,3,1,0:T(8,128)} fusion(bf16[3,18,130,320]{2,3,1,0:T(8,128)(2,1)S(1)} %copy-done.2, bf16[320,3,3,320]{3,0,2,1:T(8,128)(2,1)S(1)} %copy-done.9), kind=kOutput, calls=%fused_computation.99 | convolution fusion | flops 1258291200 | bytes 12042240 | tf_op jit(solution)/shard_map/bhwc,cd->bhwd/dot_general | solution.py:45
  131.3 5.7 %fusion.88 = f32[3,16,128,320]{2,3,1,0:T(8,128)} fusion(bf16[3,18,130,320]{2,3,1,0:T(8,128)(2,1)S(1)} %copy-done.2, bf16[320,3,3,320]{3,0,2,1:T(8,128)(2,1)S(1)} %copy-done.9), kind=kOutput, calls=%fused_computation.103 | convolution fusion | flops 1258291200 | bytes 12042240 | tf_op jit(solution)/shard_map/bhwc,cd->bhwd/dot_general | solution.py:45
  142.4 28.2 %multiply_convert_fusion.1 = (bf16[3,16,128,320]{2,3,1,0:T(8,128)(2,1)}, f32[3,16,128,320]{2,3,1,0:T(8,128)}) fusion(f32[3,320]{1,0:T(4,128)S(1)} %fusion.163, bf16[3,18,130,320]{2,3,1,0:T(8,128)(2,1)} %get-tuple-element.13, bf16[320,3,3,320]{3,0,2,1:T(8,128)(2,1)S(1)} %copy-done.9, f32[3,16,128,320]{2,3,1,0:T(8,128)} %fusion.64, ...), kind=kOutput, calls=%fused_computation.29 | convolution fusion | flops 1285816320 | bytes 78895104 | tf_op jit(solution)/shard_map/bhwc,cd->bhwd/dot_general | solution.py:45
  170.6 7.3 %multiply_convert_fusion = bf16[3,16,128,320]{2,3,1,0:T(8,128)(2,1)S(1)} fusion(f32[3,16,128,320]{2,3,1,0:T(8,128)} %get-tuple-element.21, bf16[3,16,128,320]{2,3,1,0:T(8,128)(2,1)} %param.17, bf16[320,320]{1,0:T(8,128)(2,1)S(1)} %all_gather.18), kind=kOutput, calls=%fused_computation.27 | convolution fusion | flops 1275985920 | bytes 15933440 | tf_op jit(solution)/shard_map/bhwd,cd->bhwc/dot_general | solution.py:106
  178.0 5.7 %fusion.101 = f32[320,9,320]{0,2,1:T(8,128)S(1)} fusion(bf16[3,16,128,320]{2,3,1,0:T(8,128)(2,1)S(1)} %multiply_convert_fusion, bf16[3,18,130,320]{2,3,1,0:T(8,128)(2,1)} %get-tuple-element.13), kind=kOutput, calls=%fused_computation.110 | convolution fusion | flops 1258291200 | bytes 8355840 | tf_op jit(solution)/shard_map/bhwc,bhwd->cd/dot_general | solution.py:123
  210.8 5.6 %copy.38 = f32[320,2880]{1,0:T(8,128)} copy(f32[320,2880]{0,1:T(8,128)} %bitcast.305) | data formatting | bytes 7372800 | tf_op jit(solution)/shard_map/reshape | solution.py:130
  216.4 7.6 %fusion.156 = f32[3,16,128,320]{2,3,1,0:T(8,128)} fusion(bf16[3,16,128,320]{2,3,1,0:T(8,128)(2,1)} %get-tuple-element.20, bf16[320,320]{1,0:T(8,128)(2,1)S(1)} %all_gather.18), kind=kOutput, calls=%fused_computation.151 | convolution fusion | flops 1258291200 | bytes 12001280 | tf_op jit(solution)/shard_map/bhwc,cd->bhwd/dot_general | solution.py:104
  228.7 9.0 %fusion.42 = f32[3,16,128,320]{2,3,1,0:T(8,128)} fusion(bf16[3,18,130,320]{2,3,1,0:T(8,128)(2,1)} %get-tuple-element.12, bf16[320,3,3,320]{3,0,2,1:T(8,128)(2,1)} %all-gather.4.cloned.1.call-done), kind=kOutput, calls=%fused_computation.57 | convolution fusion | flops 1258291200 | bytes 12042240 | tf_op jit(solution)/shard_map/bhwc,cd->bhwd/dot_general | solution.py:45
  237.7 7.5 %fusion.44 = f32[3,16,128,320]{2,3,1,0:T(8,128)} fusion(bf16[3,18,130,320]{2,3,1,0:T(8,128)(2,1)} %get-tuple-element.12, bf16[320,3,3,320]{3,0,2,1:T(8,128)(2,1)S(1)} %copy-done.11), kind=kOutput, calls=%fused_computation.59 | convolution fusion | flops 1258291200 | bytes 12042240 | tf_op jit(solution)/shard_map/bhwc,cd->bhwd/dot_general | solution.py:45
  250.7 5.6 %fusion.48 = f32[3,16,128,320]{2,3,1,0:T(8,128)} fusion(bf16[3,18,130,320]{2,3,1,0:T(8,128)(2,1)S(1)} %bitcast.300, bf16[320,3,3,320]{3,0,2,1:T(8,128)(2,1)S(1)} %copy-done.11), kind=kOutput, calls=%fused_computation.63 | convolution fusion | flops 1258291200 | bytes 12042240 | tf_op jit(solution)/shard_map/bhwc,cd->bhwd/dot_general | solution.py:45
  261.6 6.0 %fusion.52 = f32[3,16,128,320]{2,3,1,0:T(8,128)} fusion(bf16[3,18,130,320]{2,3,1,0:T(8,128)(2,1)S(1)} %bitcast.300, bf16[320,3,3,320]{3,0,2,1:T(8,128)(2,1)S(1)} %copy-done.11), kind=kOutput, calls=%fused_computation.67 | convolution fusion | flops 1258291200 | bytes 12042240 | tf_op jit(solution)/shard_map/bhwc,cd->bhwd/dot_general | solution.py:45
  267.6 5.6 %fusion.54 = f32[3,16,128,320]{2,3,1,0:T(8,128)} fusion(bf16[3,18,130,320]{2,3,1,0:T(8,128)(2,1)S(1)} %bitcast.300, bf16[320,3,3,320]{3,0,2,1:T(8,128)(2,1)S(1)} %copy-done.11), kind=kOutput, calls=%fused_computation.69 | convolution fusion | flops 1258291200 | bytes 12042240 | tf_op jit(solution)/shard_map/bhwc,cd->bhwd/dot_general | solution.py:45
  278.5 28.6 %add_convert_fusion = bf16[3,16,128,320]{2,3,1,0:T(8,128)(2,1)} fusion(f32[3,16,128,320]{2,3,1,0:T(8,128)} %fusion.156, f32[3,16,128,320]{2,3,1,0:T(8,128)} %fusion.42, f32[3,16,128,320]{2,3,1,0:T(8,128)} %fusion.44, f32[3,16,128,320]{2,3,1,0:T(8,128)} %fusion.46, f32[3,16,128,320]{2,3,1,0:T(8,128)} %fusion.48, f32[3,16,128,320]{2,3,1,0:T(8,128)} %fusion.50, ...), kind=kOutput, calls=%fused_computation.28 | convolution fusion | flops 1287782400 | bytes 78892800 | tf_op jit(solution)/shard_map/bhwc,cd->bhwd/dot_general | solution.py:45
  307.2 7.6 %fusion.158 = f32[3,16,128,320]{2,3,1,0:T(8,128)} fusion(bf16[3,16,128,320]{2,3,1,0:T(8,128)(2,1)} %copy-done.3, bf16[320,3,3,320]{3,0,2,1:T(8,128)(2,1)S(1)} %copy-done.9), kind=kOutput, calls=%fused_computation.153 | convolution fusion | flops 1258291200 | bytes 12042240 | tf_op jit(solution)/shard_map/bhwd,cd->bhwc/dot_general | solution.py:60
  325.4 6.3 %fusion.9 = bf16[3,18,130,320]{2,3,1,0:T(8,128)(2,1)S(1)} fusion(bf16[3,1,128,320]{2,3,1,0:T(8,128)(2,1)S(1)} %collective-permute-done.3, bf16[3,16,128,320]{2,3,1,0:T(8,128)(2,1)S(1)} %copy-done.4, bf16[3,1,128,320]{2,3,1,0:T(8,128)(2,1)S(1)} %collective-permute-done.2), kind=kLoop, calls=%fused_computation.15 | loop fusion | flops 26956800 | bytes 8916480 | tf_op jit(solution)/shard_map/concatenate | solution.py:20
  331.8 5.5 %fusion.30 = f32[3,16,128,320]{2,3,1,0:T(8,128)} fusion(bf16[3,18,130,320]{2,3,1,0:T(8,128)(2,1)S(1)} %fusion.9, bf16[320,3,3,320]{3,0,2,1:T(8,128)(2,1)S(1)} %copy-done.9), kind=kOutput, calls=%fused_computation.45 | convolution fusion | flops 1258291200 | bytes 12042240 | tf_op jit(solution)/shard_map/bhwd,cd->bhwc/dot_general | solution.py:60
  342.7 5.5 %fusion.34 = f32[3,16,128,320]{2,3,1,0:T(8,128)} fusion(bf16[3,18,130,320]{2,3,1,0:T(8,128)(2,1)S(1)} %fusion.9, bf16[320,3,3,320]{3,0,2,1:T(8,128)(2,1)S(1)} %copy-done.9), kind=kOutput, calls=%fused_computation.49 | convolution fusion | flops 1258291200 | bytes 12042240 | tf_op jit(solution)/shard_map/bhwd,cd->bhwc/dot_general | solution.py:60
  364.4 24.3 %fusion.152 = f32[16,320]{1,0:T(8,128)S(1)} fusion(f32[3,16,128,320]{2,3,1,0:T(8,128)} %fusion.28, f32[3,16,128,320]{2,3,1,0:T(8,128)} %fusion.23, f32[3,16,128,320]{2,3,1,0:T(8,128)} %fusion.30, f32[3,16,128,320]{2,3,1,0:T(8,128)} %fusion.32, f32[3,16,128,320]{2,3,1,0:T(8,128)} %fusion.158, f32[3,16,128,320]{2,3,1,0:T(8,128)} %fusion.34, ...), kind=kOutput, calls=%fused_computation.128 | convolution fusion | flops 393314304 | bytes 70823936 | tf_op jit(solution)/shard_map/bhwr,bhwc->rc/dot_general | solution.py:115
  388.7 22.2 %all-gather = f32[256,320]{1,0:T(8,128)S(1)} all-gather(f32[16,320]{1,0:T(8,128)S(1)} %fusion.152), channel_id=2, replica_groups=mesh['groups'=2,'mp'=8,'dp'=2] {'mp','dp'}, dimensions={0}, use_global_device_ids=true | all-gather | bytes 348160 | tf_op jit(solution)/shard_map/all_gather | solution.py:9
  (101 shorter events, 118.9 us)
Async XLA Ops:
  7.2 62.4 %copy-start = (bf16[1280,320]{0,1:T(8,128)(2,1)S(1)}, bf16[1280,320]{0,1:T(8,128)(2,1)}, u32[]{:S(2)}) copy-start(bf16[1280,320]{0,1:T(8,128)(2,1)} %param.13) | copy-start | bytes 2457604
  7.2 87.5 %all-gather.6.cloned.1.call-start = ((), (), s32[]{:S(2)}) async-start(), calls=%async_computation.2 | async-start | bytes 2488320 | tf_op jit(solution)/shard_map/all_gather | solution.py:99
  7.9 11.8 %copy-start.13 = (bf16[40,320]{1,0:T(8,128)(2,1)S(1)}, bf16[40,320]{1,0:T(8,128)(2,1)}, u32[]{:S(2)}) copy-start(bf16[40,320]{1,0:T(8,128)(2,1)} %param.16) | copy-start | bytes 76804
  7.9 61.5 %copy-start.15 = (s32[3]{0:T(128)S(1)}, s32[3]{0:T(128)}, u32[]{:S(2)}) copy-start(s32[3]{0:T(128)} %param.11) | copy-start | bytes 40
  7.9 220.7 %all-gather.4.cloned.1.call-start = ((), (), s32[]{:S(2)}) async-start(), calls=%async_computation.1 | async-start | bytes 2488320 | tf_op jit(solution)/shard_map/all_gather | solution.py:96
  13.5 56.4 %collective-permute-start = (bf16[2,3,1,128,320]{3,4,2,1,0:T(8,128)(2,1)S(1)}, bf16[2,3,1,128,320]{3,4,2,1,0:T(8,128)(2,1)S(1)}, u32[]{:S(2)}, u32[]{:S(2)}) collective-permute-start(bf16[2,3,1,128,320]{3,4,2,1,0:T(8,128)(2,1)S(1)} %get-tuple-element.14), channel_id=1, source_target_pairs={{0,2},{2,4},{4,6},{6,8},{8,10},{10,12},{12,14},{1,3},{3,5},{5,7},{... | collective-permute-start | bytes 1474568 | tf_op jit(solution)/shard_map/ppermute | solution.py:22
  18.3 51.5 %collective-permute-start.1 = (bf16[2,3,1,128,320]{3,4,2,1,0:T(8,128)(2,1)S(1)}, bf16[2,3,1,128,320]{3,4,2,1,0:T(8,128)(2,1)S(1)}, u32[]{:S(2)}, u32[]{:S(2)}) collective-permute-start(bf16[2,3,1,128,320]{3,4,2,1,0:T(8,128)(2,1)S(1)} %get-tuple-element.15), channel_id=1, source_target_pairs={{2,0},{4,2},{6,4},{8,6},{10,8},{12,10},{14,12},{3,1},{5,3},{7,5},{... | collective-permute-start | bytes 1474568 | tf_op jit(solution)/shard_map/ppermute | solution.py:24
  19.7 344.7 %reduce-scatter.4.cloned.1.call-start = ((), (), s32[]{:S(2)}) async-start(), calls=%async_computation.4 | async-start | bytes 4608000
  94.7 9.1 %copy-start.2 = (bf16[3,18,130,320]{2,3,1,0:T(8,128)(2,1)S(1)}, bf16[3,18,130,320]{2,3,1,0:T(8,128)(2,1)}, u32[]{:S(2)}) copy-start(bf16[3,18,130,320]{2,3,1,0:T(8,128)(2,1)} %get-tuple-element.13) | copy-start | bytes 13478404
  94.7 9.1 %copy-start.9 = (bf16[320,3,3,320]{3,0,2,1:T(8,128)(2,1)S(1)}, bf16[320,3,3,320]{3,0,2,1:T(8,128)(2,1)}, u32[]{:S(2)}) copy-start(bf16[320,3,3,320]{3,0,2,1:T(8,128)(2,1)} %all-gather.6.cloned.1.call-done) | copy-start | bytes 5529604
  177.9 28.4 %copy-start.3 = (bf16[3,16,128,320]{2,3,1,0:T(8,128)(2,1)}, bf16[3,16,128,320]{2,3,1,0:T(8,128)(2,1)S(1)}, u32[]{:S(2)}) copy-start(bf16[3,16,128,320]{2,3,1,0:T(8,128)(2,1)S(1)} %multiply_convert_fusion) | copy-start | bytes 11796484
  178.0 14.5 %slice-start.3 = ((s8[8847360]{0:T(1024)(128)(4,1)}), s8[4194304]{0:T(1024)(128)(4,1)S(1)}, s32[]{:S(2)}) async-start(s8[8847360]{0:T(1024)(128)(4,1)} %bitcast.301), calls=%async_computation.8 | async-start | bytes 8388608
  178.0 14.5 %slice-start.4 = ((s8[8847360]{0:T(1024)(128)(4,1)}), s8[4194304]{0:T(1024)(128)(4,1)S(1)}, s32[]{:S(2)}) async-start(s8[8847360]{0:T(1024)(128)(4,1)} %bitcast.301), calls=%async_computation.9 | async-start | bytes 8388608
  183.7 136.3 %collective-permute-start.2 = (bf16[3,1,128,320]{2,3,1,0:T(8,128)(2,1)S(1)}, bf16[3,1,128,320]{2,3,1,0:T(8,128)(2,1)S(1)}, u32[]{:S(2)}, u32[]{:S(2)}) collective-permute-start(bf16[3,1,128,320]{2,3,1,0:T(8,128)(2,1)S(1)} %get-tuple-element.16), channel_id=1, source_target_pairs={{0,2},{2,4},{4,6},{6,8},{8,10},{10,12},{12,14},{1,3},{3,5},{5,7},{... | collective-permute-start | bytes 737288 | tf_op jit(solution)/shard_map/ppermute | solution.py:22
  185.1 129.7 %collective-permute-start.3 = (bf16[3,1,128,320]{2,3,1,0:T(8,128)(2,1)S(1)}, bf16[3,1,128,320]{2,3,1,0:T(8,128)(2,1)S(1)}, u32[]{:S(2)}, u32[]{:S(2)}) collective-permute-start(bf16[3,1,128,320]{2,3,1,0:T(8,128)(2,1)S(1)} %get-tuple-element.17), channel_id=1, source_target_pairs={{2,0},{4,2},{6,4},{8,6},{10,8},{12,10},{14,12},{3,1},{5,3},{7,5},{... | collective-permute-start | bytes 737288 | tf_op jit(solution)/shard_map/ppermute | solution.py:24
  216.4 7.6 %copy-start.7 = (bf16[3,16,128,320]{2,3,1,0:T(8,128)(2,1)S(1)}, bf16[3,16,128,320]{2,3,1,0:T(8,128)(2,1)}, u32[]{:S(2)}) copy-start(bf16[3,16,128,320]{2,3,1,0:T(8,128)(2,1)} %get-tuple-element.20) | copy-start | bytes 11796484
  216.4 7.6 %copy-start.14 = (bf16[3,16,128,320]{2,3,1,0:T(8,128)(2,1)S(1)}, bf16[3,16,128,320]{2,3,1,0:T(8,128)(2,1)}, u32[]{:S(2)}) copy-start(bf16[3,16,128,320]{2,3,1,0:T(8,128)(2,1)} %param.17) | copy-start | bytes 11796484
  228.6 182.9 %all-reduce.5.cloned.1.call-start = ((), (), s32[]{:S(2)}) async-start(), calls=%async_computation.3 | async-start | bytes 1024000 | tf_op jit(solution)/shard_map/psum | solution.py:134
  228.7 9.0 %copy-start.11 = (bf16[320,3,3,320]{3,0,2,1:T(8,128)(2,1)S(1)}, bf16[320,3,3,320]{3,0,2,1:T(8,128)(2,1)}, u32[]{:S(2)}) copy-start(bf16[320,3,3,320]{3,0,2,1:T(8,128)(2,1)} %all-gather.4.cloned.1.call-done) | copy-start | bytes 5529604
  228.7 16.5 %slice-start = ((s8[8847360]{0:T(1024)(128)(4,1)}), s8[4194304]{0:T(1024)(128)(4,1)S(1)}, s32[]{:S(2)}) async-start(s8[8847360]{0:T(1024)(128)(4,1)} %bitcast.299), calls=%async_computation.5 | async-start | bytes 8388608
  228.7 16.5 %slice-start.1 = ((s8[8847360]{0:T(1024)(128)(4,1)}), s8[4194304]{0:T(1024)(128)(4,1)S(1)}, s32[]{:S(2)}) async-start(s8[8847360]{0:T(1024)(128)(4,1)} %bitcast.299), calls=%async_computation.6 | async-start | bytes 8388608
  237.7 7.5 %slice-start.2 = ((s8[8847360]{0:T(1024)(128)(4,1)}), s8[458752]{0:T(1024)(128)(4,1)S(1)}, s32[]{:S(2)}) async-start(s8[8847360]{0:T(1024)(128)(4,1)} %bitcast.299), calls=%async_computation.7 | async-start | bytes 917504
  307.2 7.6 %copy-start.4 = (bf16[3,16,128,320]{2,3,1,0:T(8,128)(2,1)S(1)}, bf16[3,16,128,320]{2,3,1,0:T(8,128)(2,1)}, u32[]{:S(2)}) copy-start(bf16[3,16,128,320]{2,3,1,0:T(8,128)(2,1)} %copy-done.3) | copy-start | bytes 11796484
  364.4 51.0 %copy-start.1 = (bf16[1280,320]{0,1:T(8,128)(2,1)S(1)}, bf16[1280,320]{0,1:T(8,128)(2,1)}, u32[]{:S(2)}) copy-start(bf16[1280,320]{0,1:T(8,128)(2,1)} %param.13) | copy-start | bytes 2457604
  (6 other events, 22.7 us)
Sparse Core Ops, SparseCore 0:
  10.2 66.9 all-gather.5
  79.4 49.2 all-gather.3
  228.7 87.1 reduce-scatter.3
  364.5 20.1 all-reduce.4
